TPU v7x, 32 devices: a whole 2x2x4 slice. The times are simulated.
32 devices in a mesh: seq: 16 (over z, x, core), tp: 2 (over y).
Axes of the slice: x: 2, y: 2, z: 4, core: 2. Of those that a mesh axis runs over, the one named last changes fastest.
Arguments:
- q_feat: bfloat16 [4096, 4096], P('seq', 'tp'), may hold values from -6 to 6
- k_feat: bfloat16 [4096, 4096], P('seq', 'tp'), may hold values from -6 to 6
- v_feat: bfloat16 [4096, 4096], P('seq', 'tp'), may hold values from -6 to 6
- stream: bfloat16 [4096, 4096], P('seq', 'tp'), may hold values from -6 to 6
- filters: float32 [4096, 4096], P(('tp', 'seq')), may hold values from -1.2 to 1.2
- w_out: bfloat16 [4096, 4096], P('tp', 'seq'), may hold values from -0.125 to 0.125
Outputs:
- mixed_out: bfloat16 [4096, 4096], P('seq', 'tp')
All inputs are finite; a program needn't handle non-finite values.
Results may differ from a plain program's by a relative error of at most 0.012.
Values may be sent and summed in bfloat16 or wider, within the bound.
A program may use at most 128 MiB of HBM per device.

v0:
```python
import functools
import math

import jax
import jax.numpy as jnp
import numpy as np
from jax import lax
from jax.experimental import pallas as pl
from jax.experimental.pallas import tpu as pltpu
from jax.sharding import PartitionSpec as P

LANES = 128
GROUP = 16

def window_extent(total):
    chosen = 2
    for normalizing_multiplier in range(2, math.isqrt(total) + 1, 2):
        if total % normalizing_multiplier == 0:
            chosen = normalizing_multiplier
    return chosen


def make_tables(first, second, total):
    rows = jnp.arange(first, dtype=jnp.int32)
    half_rows = jnp.arange(first // 2, dtype=jnp.int32)
    columns = jnp.arange(second, dtype=jnp.int32)
    angle_one = (
        2.0 * math.pi / first * (rows[:, None] * half_rows[None, :] % first).astype(jnp.float32)
    )
    angle_two = (
        2.0 * math.pi / second * (columns[:, None] * columns[None, :] % second).astype(jnp.float32)
    )
    angle_twist = (
        2.0 * math.pi / total * (rows[:, None] * columns[None, :] % total).astype(jnp.float32)
    )
    return (
        jnp.cos(angle_one),
        jnp.sin(angle_one),
        jnp.cos(angle_two),
        jnp.sin(angle_two),
        jnp.cos(angle_twist),
        jnp.sin(angle_twist),
    )


def forward_transform(signal, tables, first, second):
    cosine_first, sin_one, cos_two, sin_two, cos_twist, sin_twist = tables
    chans = signal.shape[0]
    shaped = signal.reshape(chans, first // 2, second)
    highest = lax.Precision.HIGHEST
    real_a = jnp.einsum("kn,cnm->ckm", cosine_first, shaped, precision=highest)
    imaginary_left = -jnp.einsum("kn,cnm->ckm", sin_one, shaped, precision=highest)
    real_b = real_a * cos_twist + imaginary_left * sin_twist
    imag_b = imaginary_left * cos_twist - real_a * sin_twist
    real_x = jnp.einsum("ckn,nm->ckm", real_b, cos_two, precision=highest) + jnp.einsum(
        "ckn,nm->ckm", imag_b, sin_two, precision=highest
    )
    imag_x = jnp.einsum("ckn,nm->ckm", imag_b, cos_two, precision=highest) - jnp.einsum(
        "ckn,nm->ckm", real_b, sin_two, precision=highest
    )
    return (real_x, imag_x)


def inverse_transform(real_p, imag_p, tables, first, second):
    cosine_first, sin_one, cos_two, sin_two, cos_twist, sin_twist = tables
    highest = lax.Precision.HIGHEST
    real_d = jnp.einsum("ckn,nm->ckm", real_p, cos_two, precision=highest) - jnp.einsum(
        "ckn,nm->ckm", imag_p, sin_two, precision=highest
    )
    imag_d = jnp.einsum("ckn,nm->ckm", real_p, sin_two, precision=highest) + jnp.einsum(
        "ckn,nm->ckm", imag_p, cos_two, precision=highest
    )
    kernel_spectrum_real = real_d * cos_twist - imag_d * sin_twist
    imag_e = real_d * sin_twist + imag_d * cos_twist
    result = jnp.einsum(
        "kn,ckm->cnm", cosine_first, kernel_spectrum_real, precision=highest
    ) - jnp.einsum("kn,ckm->cnm", sin_one, imag_e, precision=highest)
    return result / (first * second)


def long_conv(mixed_cols, filters):
    chans, length = filters.shape
    total = 2 * length
    first = window_extent(total)
    second = total // first
    tables = make_tables(first, second, total)
    stacked = jnp.concatenate([mixed_cols.astype(jnp.float32), filters], axis=0)
    real_x, imag_x = forward_transform(stacked, tables, first, second)
    real_p = real_x[:chans] * real_x[chans:] - imag_x[:chans] * imag_x[chans:]
    imag_p = real_x[:chans] * imag_x[chans:] + imag_x[:chans] * real_x[chans:]
    result = inverse_transform(real_p, imag_p, tables, first, second)
    return result.reshape(chans, length)


def spectral_tables(length):
    total = 2 * length
    first = total // LANES
    slots = first // 2
    n_one = np.arange(slots)
    base = np.zeros((slots, 2, slots))
    for s in range(1, slots):
        angle = 2.0 * np.pi * (s * n_one % first) / first
        base[s, 0] = np.cos(angle)
        base[s, 1] = -np.sin(angle)
    base[0, 0] = 1.0
    base[0, 1] = 1.0 - 2.0 * (n_one % 2)
    outer = np.kron(base.reshape(first, slots), np.eye(GROUP))
    n_two = np.arange(LANES)
    k_two = np.arange(LANES)
    inner = np.zeros((slots, 2 * LANES, 2 * LANES))

    def wave(k_one, rows):
        turns = (first * rows[:, None] + k_one) * n_two[None, :] % total
        return np.exp(-2j * np.pi * turns / total)

    for s in range(1, slots):
        t = wave(s, k_two)
        inner[s] = np.block([[t.real, -t.imag], [t.imag, t.real]])
    half = LANES // 2
    zero = wave(0, k_two[:half])
    mid = wave(slots, k_two[:half])
    inner[0, :half, :LANES] = zero.real
    inner[0, half:LANES, LANES:] = mid.real
    inner[0, LANES : LANES + half, :LANES] = zero.imag
    inner[0, LANES + half :, LANES:] = mid.imag
    inner[0, LANES, :LANES] = 1.0 - 2.0 * (n_two % 2)
    cast = lambda a: np.ascontiguousarray(a).astype(jnp.bfloat16)
    return cast(outer), cast(outer.T), cast(inner), cast(inner.transpose(0, 2, 1))


def spectral_product(a, b, slot_zero):
    a_re, a_im = a[:LANES], a[LANES:]
    b_re, b_im = b[:LANES], b[LANES:]
    rr, ii = a_re * b_re, a_im * b_im
    p_re = rr - ii
    p_im = a_re * b_im + a_im * b_re
    if slot_zero:
        top = lax.broadcasted_iota(jnp.int32, p_re.shape, 0) == 0
        p_re = jnp.where(top, 0.5 * rr, p_re)
        p_im = jnp.where(top, 0.5 * ii, p_im)
    return jnp.concatenate([p_re, p_im], axis=0)


def mixer_kernel(
    peers,
    k_ref,
    v_ref,
    q_ref,
    taps_ref,
    outer_ref,
    outer_t_ref,
    inner_ref,
    inner_t_ref,
    gated_ref,
    sent,
    signal,
    result,
    returned,
    turned,
    spectrum,
    work,
    send_one,
    recv_one,
    send_two,
    recv_two,
):
    me = lax.axis_index("seq")
    rows = k_ref.shape[0]
    slots = signal.shape[0]
    per = slots // peers
    total = 2 * slots * LANES

    barrier = pltpu.get_barrier_semaphore()
    for i in range(1, peers):
        pl.semaphore_signal(
            barrier,
            inc=1,
            device_id={"seq": lax.rem(me + i, peers)},
            device_id_type=pl.DeviceIdType.MESH,
        )

    def mix(p, carry):
        cols = pl.ds(pl.multiple_of(p * LANES, LANES), LANES)
        product = k_ref[:, cols].astype(jnp.float32) * v_ref[:, cols].astype(jnp.float32)
        sent[p] = product.astype(jnp.bfloat16).reshape(per, LANES, LANES)
        return carry

    lax.fori_loop(0, peers, mix, 0)
    pl.semaphore_wait(barrier, peers - 1)

    first_copies = []
    for i in range(1, peers):
        target = lax.rem(me + i, peers)
        copy = pltpu.make_async_remote_copy(
            src_ref=sent.at[target],
            dst_ref=signal.at[pl.ds(me * per, per)],
            send_sem=send_one.at[i],
            recv_sem=recv_one.at[i],
            device_id={"seq": target},
            device_id_type=pl.DeviceIdType.MESH,
        )
        copy.start()
        first_copies.append(copy)
    signal[pl.ds(me * per, per)] = sent[me]

    def outer_stage(source):
        def step(g, carry):
            lo = pl.ds(pl.multiple_of(g * 2 * GROUP, 2 * GROUP), GROUP)
            hi = pl.ds(pl.multiple_of(g * 2 * GROUP + GROUP, GROUP), GROUP)
            block = jnp.concatenate(
                [
                    source[:, lo, :].reshape(slots * GROUP, LANES),
                    source[:, hi, :].reshape(slots * GROUP, LANES),
                ],
                axis=1,
            )
            y = jnp.dot(outer_ref[...], block, preferred_element_type=jnp.float32)
            y = y.astype(jnp.bfloat16)
            work[:, :, lo, :] = y[:, :LANES].reshape(slots, 2, GROUP, LANES)
            work[:, :, hi, :] = y[:, LANES:].reshape(slots, 2, GROUP, LANES)
            return carry

        lax.fori_loop(0, LANES // (2 * GROUP), step, 0)

    def inner_forward(s):
        return jnp.dot(
            inner_ref[s],
            work[s].reshape(2 * LANES, LANES),
            preferred_element_type=jnp.float32,
        )

    def turn(n, carry):
        cols = pl.ds(pl.multiple_of(n * LANES, LANES), LANES)
        turned[n] = taps_ref[:, cols].T.astype(jnp.bfloat16)
        return carry

    lax.fori_loop(0, slots, turn, 0)
    outer_stage(turned)

    def tap_step(s, carry):
        spectrum[s] = inner_forward(s)
        return carry

    lax.fori_loop(0, slots, tap_step, 0, unroll=2)

    for copy in first_copies:
        copy.wait_recv()
    outer_stage(signal)

    def middle(s, slot_zero):
        p = spectral_product(inner_forward(s), spectrum[s], slot_zero)
        q = jnp.dot(inner_t_ref[s], p.astype(jnp.bfloat16), preferred_element_type=jnp.float32)
        work[s] = q.astype(jnp.bfloat16).reshape(2, LANES, LANES)

    middle(0, True)

    def middle_step(s, carry):
        middle(s, False)
        return carry

    lax.fori_loop(1, slots, middle_step, 0, unroll=2)

    def outer_back(g, carry):
        lo = pl.ds(pl.multiple_of(g * 2 * GROUP, 2 * GROUP), GROUP)
        hi = pl.ds(pl.multiple_of(g * 2 * GROUP + GROUP, GROUP), GROUP)
        block = jnp.concatenate(
            [
                work[:, :, lo, :].reshape(2 * slots * GROUP, LANES),
                work[:, :, hi, :].reshape(2 * slots * GROUP, LANES),
            ],
            axis=1,
        )
        y = jnp.dot(outer_t_ref[...], block, preferred_element_type=jnp.float32)
        y = (y * (2.0 / total)).astype(jnp.bfloat16)
        result[:, lo, :] = y[:, :LANES].reshape(slots, GROUP, LANES)
        result[:, hi, :] = y[:, LANES:].reshape(slots, GROUP, LANES)
        return carry

    lax.fori_loop(0, LANES // (2 * GROUP), outer_back, 0)

    second_copies = []
    for i in range(1, peers):
        target = lax.rem(me + i, peers)
        copy = pltpu.make_async_remote_copy(
            src_ref=result.at[pl.ds(target * per, per)],
            dst_ref=returned.at[me],
            send_sem=send_two.at[i],
            recv_sem=recv_two.at[i],
            device_id={"seq": target},
            device_id_type=pl.DeviceIdType.MESH,
        )
        copy.start()
        second_copies.append(copy)

    def gate(p, block):
        cols = pl.ds(pl.multiple_of(p * LANES, LANES), LANES)
        conv = block.reshape(rows, LANES).astype(jnp.float32)
        gated_ref[:, cols] = (q_ref[:, cols].astype(jnp.float32) * conv).astype(jnp.bfloat16)

    gate(me, result[pl.ds(me * per, per)])
    for i, copy in enumerate(second_copies, 1):
        copy.wait_recv()
        source = lax.rem(me + peers - i, peers)
        gate(source, returned[source])
    for copy in first_copies + second_copies:
        copy.wait_send()


def gated_mixer(q_feat, k_feat, v_feat, filters, peers):
    rows, columns = q_feat.shape
    chans, length = filters.shape
    slots = length // LANES
    per = rows // LANES
    tables = spectral_tables(length)
    vmem = pl.BlockSpec(memory_space=pltpu.VMEM)
    bf16 = jnp.bfloat16
    return pl.pallas_call(
        functools.partial(mixer_kernel, peers),
        out_shape=jax.ShapeDtypeStruct((rows, columns), bf16),
        in_specs=[vmem] * 8,
        out_specs=vmem,
        scratch_shapes=[
            pltpu.VMEM((peers, per, LANES, LANES), bf16),
            pltpu.VMEM((slots, LANES, LANES), bf16),
            pltpu.VMEM((slots, LANES, LANES), bf16),
            pltpu.VMEM((peers, per, LANES, LANES), bf16),
            pltpu.VMEM((slots, LANES, LANES), bf16),
            pltpu.VMEM((slots, 2 * LANES, LANES), jnp.float32),
            pltpu.VMEM((slots, 2, LANES, LANES), bf16),
            pltpu.SemaphoreType.DMA((peers,)),
            pltpu.SemaphoreType.DMA((peers,)),
            pltpu.SemaphoreType.DMA((peers,)),
            pltpu.SemaphoreType.DMA((peers,)),
        ],
        compiler_params=pltpu.CompilerParams(
            collective_id=0, has_side_effects=True, vmem_limit_bytes=48 * 1024 * 1024
        ),
        cost_estimate=pl.CostEstimate(
            flops=40 * 1024 * 1024 * slots * chans // 8,
            bytes_accessed=16 * 1024 * 1024,
            transcendentals=0,
        ),
    )(k_feat, v_feat, q_feat, filters, *[jnp.asarray(t) for t in tables])


def gated_features(q_feat, k_feat, v_feat, filters):
    peers = lax.axis_size("seq")
    if filters.shape[0] == LANES and q_feat.shape[0] % LANES == 0:
        return gated_mixer(q_feat, k_feat, v_feat, filters, peers)
    mixed = (k_feat.astype(jnp.float32) * v_feat.astype(jnp.float32)).astype(jnp.bfloat16)
    sent_mixed = lax.all_to_all(mixed.T, "seq", split_axis=0, concat_axis=1, tiled=True)
    conv_out = long_conv(sent_mixed, filters).astype(jnp.bfloat16)
    returned_output = lax.all_to_all(conv_out, "seq", split_axis=1, concat_axis=0, tiled=True)
    return (q_feat.astype(jnp.float32) * returned_output.T.astype(jnp.float32)).astype(
        jnp.bfloat16
    )


def local(q_feat, k_feat, v_feat, stream, filters, w_out):
    gated = gated_features(q_feat, k_feat, v_feat, filters)
    terms = jnp.dot(
        gated, lax.all_gather(w_out, "seq", axis=1, tiled=True), preferred_element_type=jnp.float32
    )
    accumulated_total = lax.psum_scatter(
        terms.astype(jnp.bfloat16), "tp", scatter_dimension=1, tiled=True
    ).astype(jnp.float32)
    return (stream.astype(jnp.float32) + accumulated_total).astype(jnp.bfloat16)


def solution(mesh):
    return jax.shard_map(
        local,
        mesh=mesh,
        in_specs=(
            P("seq", "tp"),
            P("seq", "tp"),
            P("seq", "tp"),
            P("seq", "tp"),
            P(("tp", "seq"), None),
            P("tp", "seq"),
        ),
        out_specs=P("seq", "tp"),
        check_vma=False,
    )
```

profile of v0, /device:TPU:18, one launch (start us, length us, event | category | flops | bytes accessed | tf_op | source)
XLA Modules:
  0.0 229.4 jit_solution(888745981047738211)
XLA Ops:
  6.5 0.0 all-gather.2.cloned.1.call-start
  6.5 0.7 all-gather.2.cloned.1.call-update
  7.3 0.0 reduce-scatter.2.cloned.1.call-start
  7.3 0.0 copy-start
  7.3 1.2 copy-done
  8.5 0.0 copy-start.1
  8.5 1.2 copy-done.1
  9.8 0.0 copy-start.2
  9.8 1.2 copy-done.2
  11.0 0.0 copy-start.3
  11.0 1.2 copy-done.3
  12.2 85.8 %shard_map.100 = bf16[256,2048]{1,0:T(8,128)(2,1)S(1)} custom-call(bf16[256,2048]{1,0:T(8,128)(2,1)S(1)} %copy-done, bf16[256,2048]{1,0:T(8,128)(2,1)S(1)} %copy-done.1, bf16[256,2048]{1,0:T(8,128)(2,1)S(1)} %copy-done.2, f32[128,4096]{1,0:T(8,128)} %taps_ref.1, bf16[1024,512]{1,0:T(8,128)(2,1)S(1)} %copy-done.3, ...), custom_call_target="tpu_custom_call" | custom-call | flops 21474836480 | bytes 16777216 | tf_op jit(solution)/shard_map/pallas_call | solution.py:317
  98.0 0.0 copy-start.4
  98.0 78.5 %all-gather.2.cloned.1.call-done = bf16[2048,4096]{1,0:T(8,128)(2,1)} async-done(((bf16[2048,256]{1,0:T(8,128)(2,1)}), bf16[2048,4096]{1,0:T(8,128)(2,1)}) %all-gather.2.cloned.1.call-update) | async-done | bytes 16777232 | tf_op jit(solution)/shard_map/all_gather | solution.py:362
  176.5 11.5 %convolution_convert_fusion = bf16[256,4096]{1,0:T(8,128)(2,1)} fusion(bf16[256,2048]{1,0:T(8,128)(2,1)S(1)} %shard_map.100, bf16[2048,4096]{1,0:T(8,128)(2,1)} %all-gather.2.cloned.1.call-done), kind=kOutput, calls=%fused_computation | convolution fusion | flops 4296015872 | bytes 19922944 | tf_op jit(solution)/shard_map/dot_general | solution.py:361
  188.0 0.0 reduce-scatter.2.cloned.1.call-update
  188.0 32.0 %reduce-scatter.2.cloned.1.call-done = bf16[256,2048]{1,0:T(8,128)(2,1)} async-done(((bf16[256,4096]{1,0:T(8,128)(2,1)}), bf16[256,2048]{1,0:T(8,128)(2,1)}) %reduce-scatter.2.cloned.1.call-update) | async-done | bytes 1048592 | tf_op jit(solution)/shard_map/reduce_scatter | solution.py:364
  220.0 0.0 copy-done.4
  220.0 2.6 %add_convert_fusion = bf16[256,2048]{1,0:T(8,128)(2,1)} fusion(bf16[256,2048]{1,0:T(8,128)(2,1)} %reduce-scatter.2.cloned.1.call-done, bf16[256,2048]{1,0:T(8,128)(2,1)S(1)} %copy-done.4), kind=kLoop, calls=%fused_computation.1 | loop fusion | flops 2097152 | bytes 3145728 | tf_op jit(solution)/shard_map/convert_element_type | solution.py:367
Async XLA Ops:
  6.5 169.9 %all-gather.2.cloned.1.call-start = ((), (), s32[]{:S(2)}) async-start(), calls=%async_computation.1 | async-start | bytes 17825792 | tf_op jit(solution)/shard_map/all_gather | solution.py:362
  7.3 212.7 %reduce-scatter.2.cloned.1.call-start = ((), (), s32[]{:S(2)}) async-start(), calls=%async_computation.2 | async-start | bytes 3145728 | tf_op jit(solution)/shard_map/reduce_scatter | solution.py:364
  7.3 1.2 copy-start
  8.5 1.2 copy-start.1
  9.8 1.2 copy-start.2
  11.0 1.2 copy-start.3
  98.0 122.0 %copy-start.4 = (bf16[256,2048]{1,0:T(8,128)(2,1)S(1)}, bf16[256,2048]{1,0:T(8,128)(2,1)}, u32[]{:S(2)}) copy-start(bf16[256,2048]{1,0:T(8,128)(2,1)} %param.13) | copy-start | bytes 3145732
Sparse Core Ops, SparseCore 0:
  9.5 166.9 all-gather.1
  188.1 31.8 reduce-scatter.1
where the time goes:
time: 231 us; the launch traced here: 229 us
  waiting for transfers between devices  111 us (48%)
  Pallas kernels  85.8 us (37%)
  between operations  13.4 us (6%)
  matrix products  11.5 us (5%)
  local copies, waits for them, and re-layouts  4.9 us (2%)
  other arithmetic  2.58 us (1%)
    pallas_call x1, Pallas kernels, gated_mixer(): pl.pallas_call(functools.partial(mixer_kernel, peers), out_shape=jax.Shap...  85.8 us
    all_gather x1, waiting for transfers between devices, local(): lax.all_gather(w_out, 'seq', axis=1, tiled=True)  78.5 us
    reduce_scatter x1, waiting for transfers between devices, local(): lax.psum_scatter(terms.astype(jnp.bfloat16), 'tp', scatter_dimension=1, t...  32 us
    dot_general x1, matrix products, local(): jnp.dot(gated, lax.all_gather(w_out, 'seq', axis=1, tiled=True), preferre...  11.5 us
    unnamed x10, local copies, waits for them, and re-layouts  4.9 us
  transfers between devices with their start and end apart: 2, of which 2 were waited for; matrix products, arithmetic and copies ran while one was open for 0% of the time, Pallas kernels for 37%

commit v1 on v0

--- a/solution.py
+++ b/solution.py
@@ -145,13 +145,22 @@
     peers,
     k_ref,
     v_ref,
+    q_hbm,
+    stream_hbm,
+    taps_hbm,
+    weights_hbm,
+    outer_hbm,
+    outer_t_hbm,
+    inner_hbm,
+    inner_t_hbm,
+    out_ref,
     q_ref,
+    stream_ref,
     taps_ref,
     outer_ref,
     outer_t_ref,
     inner_ref,
     inner_t_ref,
-    gated_ref,
     sent,
     signal,
     result,
@@ -159,16 +168,156 @@
     turned,
     spectrum,
     work,
+    gated,
+    weights,
+    kept,
+    shares,
+    arrived,
+    load_sem,
     send_one,
     recv_one,
     send_two,
     recv_two,
+    send_weight,
+    recv_weight,
+    send_share,
+    recv_share,
 ):
     me = lax.axis_index("seq")
+    tp = lax.axis_index("tp")
     rows = k_ref.shape[0]
     slots = signal.shape[0]
     per = slots // peers
     total = 2 * slots * LANES
+    mesh_ids = pl.DeviceIdType.MESH
+    depth = peers // 4
+    half = peers // 2
+    layer, side, core = me // 4, (me // 2) % 2, me % 2
+
+    loads = [
+        pltpu.make_async_copy(source, target, load_sem.at[i])
+        for i, (source, target) in enumerate(
+            [
+                (weights_hbm, weights.at[me]),
+                (taps_hbm, taps_ref),
+                (outer_hbm, outer_ref),
+                (inner_hbm, inner_ref),
+                (inner_t_hbm, inner_t_ref),
+                (outer_t_hbm, outer_t_ref),
+                (q_hbm, q_ref),
+                (stream_hbm, stream_ref),
+            ]
+        )
+    ]
+    for load in loads:
+        load.start()
+
+    def block_at(zz, xx, cc):
+        return (zz * 2 + xx) * 2 + cc
+
+    def weight_copy(block, target, way):
+        return pltpu.make_async_remote_copy(
+            src_ref=weights.at[block],
+            dst_ref=weights.at[block],
+            send_sem=send_weight.at[block, way],
+            recv_sem=recv_weight.at[block],
+            device_id={"seq": target},
+            device_id_type=mesh_ids,
+        )
+
+    to_core = block_at(layer, side, 1 - core)
+    to_side = block_at(layer, 1 - side, core)
+
+    def act(copy, sending):
+        if sending:
+            copy.start()
+        else:
+            copy.wait_send()
+
+    def spread(block, sending, up, down):
+        if up:
+
+            @pl.when(layer + 1 < depth)
+            def _():
+                act(weight_copy(block, me + 4, 2), sending)
+
+        if down:
+
+            @pl.when(layer > 0)
+            def _():
+                act(weight_copy(block, me - 4, 3), sending)
+
+        act(weight_copy(block, to_side, 1), sending)
+        act(weight_copy(block, to_core, 0), sending)
+
+    def arrive(block):
+        weight_copy(block, to_core, 0).wait_recv()
+
+    def at_distance(d, body):
+        for sign in (-1, 1) if d else (1,):
+            zz = layer + sign * d
+
+            @pl.when((zz >= 0) & (zz < depth))
+            def _():
+                body(zz, sign)
+
+    def from_layer(d):
+        if d >= depth:
+            return
+
+        def body(zz, sign):
+            block = block_at(zz, side, core)
+            arrive(block)
+            spread(block, True, sign < 0, sign > 0)
+
+        at_distance(d, body)
+
+    def from_side(d):
+        if d >= depth:
+            return
+
+        def body(zz, sign):
+            block = block_at(zz, 1 - side, core)
+            arrive(block)
+            weight_copy(block, to_core, 0).start()
+
+        at_distance(d, body)
+
+    def share_copy(b):
+        return pltpu.make_async_remote_copy(
+            src_ref=shares.at[b],
+            dst_ref=arrived.at[b],
+            send_sem=send_share.at[b],
+            recv_sem=recv_share.at[b],
+            device_id={"tp": 1 - tp},
+            device_id_type=mesh_ids,
+        )
+
+    def project(d):
+        def body(zz, sign):
+            for xx in (0, 1):
+                arrive(block_at(zz, xx, 1 - core))
+
+            def step(i, carry):
+                block = zz * 4 + i
+                terms = jnp.dot(gated[...], weights[block], preferred_element_type=jnp.float32)
+                b = block % half
+
+                @pl.when(block // half == tp)
+                def _():
+                    kept[b] = terms
+
+                @pl.when(block // half != tp)
+                def _():
+                    shares[b] = terms.astype(jnp.bfloat16)
+                    share_copy(b).start()
+
+                return carry
+
+            lax.fori_loop(0, 4, step, 0)
+
+        if d < depth:
+            at_distance(d, body)
 
     barrier = pltpu.get_barrier_semaphore()
     for i in range(1, peers):
@@ -176,8 +325,9 @@
             barrier,
             inc=1,
             device_id={"seq": lax.rem(me + i, peers)},
-            device_id_type=pl.DeviceIdType.MESH,
-        )
+            device_id_type=mesh_ids,
+        )
+    pl.semaphore_signal(barrier, inc=1, device_id={"tp": 1 - tp}, device_id_type=mesh_ids)
 
     def mix(p, carry):
         cols = pl.ds(pl.multiple_of(p * LANES, LANES), LANES)
@@ -186,7 +336,7 @@
         return carry
 
     lax.fori_loop(0, peers, mix, 0)
-    pl.semaphore_wait(barrier, peers - 1)
+    pl.semaphore_wait(barrier, peers)
 
     first_copies = []
     for i in range(1, peers):
@@ -197,11 +347,13 @@
             send_sem=send_one.at[i],
             recv_sem=recv_one.at[i],
             device_id={"seq": target},
-            device_id_type=pl.DeviceIdType.MESH,
+            device_id_type=mesh_ids,
         )
         copy.start()
         first_copies.append(copy)
     signal[pl.ds(me * per, per)] = sent[me]
+    loads[0].wait()
+    spread(me, True, True, True)
 
     def outer_stage(source):
         def step(g, carry):
@@ -234,8 +386,11 @@
         turned[n] = taps_ref[:, cols].T.astype(jnp.bfloat16)
         return carry
 
+    loads[1].wait()
     lax.fori_loop(0, slots, turn, 0)
+    loads[2].wait()
     outer_stage(turned)
+    loads[3].wait()
 
     def tap_step(s, carry):
         spectrum[s] = inner_forward(s)
@@ -246,6 +401,8 @@
     for copy in first_copies:
         copy.wait_recv()
     outer_stage(signal)
+    from_layer(1)
+    loads[4].wait()
 
     def middle(s, slot_zero):
         p = spectral_product(inner_forward(s), spectrum[s], slot_zero)
@@ -259,6 +416,8 @@
         return carry
 
     lax.fori_loop(1, slots, middle_step, 0, unroll=2)
+
+    loads[5].wait()
 
     def outer_back(g, carry):
         lo = pl.ds(pl.multiple_of(g * 2 * GROUP, 2 * GROUP), GROUP)
@@ -287,39 +446,91 @@
             send_sem=send_two.at[i],
             recv_sem=recv_two.at[i],
             device_id={"seq": target},
-            device_id_type=pl.DeviceIdType.MESH,
+            device_id_type=mesh_ids,
         )
         copy.start()
         second_copies.append(copy)
+    from_side(0)
+    from_layer(2)
+    from_side(1)
+    loads[6].wait()
 
     def gate(p, block):
         cols = pl.ds(pl.multiple_of(p * LANES, LANES), LANES)
         conv = block.reshape(rows, LANES).astype(jnp.float32)
-        gated_ref[:, cols] = (q_ref[:, cols].astype(jnp.float32) * conv).astype(jnp.bfloat16)
+        gated[:, cols] = (q_ref[:, cols].astype(jnp.float32) * conv).astype(jnp.bfloat16)
 
     gate(me, result[pl.ds(me * per, per)])
     for i, copy in enumerate(second_copies, 1):
         copy.wait_recv()
         source = lax.rem(me + peers - i, peers)
         gate(source, returned[source])
+    project(0)
+    from_layer(3)
+    from_side(2)
+    project(1)
+    project(2)
+    for d in range(3, depth):
+        if d > 3:
+            from_layer(d)
+        from_side(d)
+        project(d)
+
+    loads[7].wait()
+    width = kept.shape[2]
+
+    def finish(b, carry):
+        share_copy(b).wait_recv()
+        cols = pl.ds(pl.multiple_of(b * width, width), width)
+        added = kept[b] + arrived[b].astype(jnp.float32)
+        out_ref[:, cols] = (stream_ref[:, cols].astype(jnp.float32) + added).astype(jnp.bfloat16)
+        return carry
+
+    lax.fori_loop(0, half, finish, 0)
+
     for copy in first_copies + second_copies:
         copy.wait_send()
-
-
-def gated_mixer(q_feat, k_feat, v_feat, filters, peers):
+    spread(me, False, True, True)
+    for d in range(depth):
+
+        def settle(zz, sign):
+            if d:
+                spread(block_at(zz, side, core), False, sign < 0, sign > 0)
+            weight_copy(block_at(zz, 1 - side, core), to_core, 0).wait_send()
+
+        at_distance(d, settle)
+
+    def sent_share(b, carry):
+        share_copy(b).wait_send()
+        return carry
+
+    lax.fori_loop(0, half, sent_share, 0)
+
+
+def fused_mixer(q_feat, k_feat, v_feat, stream, filters, w_out, peers):
     rows, columns = q_feat.shape
     chans, length = filters.shape
     slots = length // LANES
     per = rows // LANES
     tables = spectral_tables(length)
     vmem = pl.BlockSpec(memory_space=pltpu.VMEM)
+    anywhere = pl.BlockSpec(memory_space=pl.ANY)
     bf16 = jnp.bfloat16
+    depth, width = w_out.shape
+    half = peers // 2
+    dma = pltpu.SemaphoreType.DMA
     return pl.pallas_call(
         functools.partial(mixer_kernel, peers),
         out_shape=jax.ShapeDtypeStruct((rows, columns), bf16),
-        in_specs=[vmem] * 8,
+        in_specs=[vmem] * 2 + [anywhere] * 8,
         out_specs=vmem,
         scratch_shapes=[
+            pltpu.VMEM((rows, columns), bf16),
+            pltpu.VMEM((rows, columns), bf16),
+            pltpu.VMEM((chans, length), jnp.float32),
+        ]
+        + [pltpu.VMEM(t.shape, bf16) for t in tables]
+        + [
             pltpu.VMEM((peers, per, LANES, LANES), bf16),
             pltpu.VMEM((slots, LANES, LANES), bf16),
             pltpu.VMEM((slots, LANES, LANES), bf16),
@@ -327,26 +538,33 @@
             pltpu.VMEM((slots, LANES, LANES), bf16),
             pltpu.VMEM((slots, 2 * LANES, LANES), jnp.float32),
             pltpu.VMEM((slots, 2, LANES, LANES), bf16),
-            pltpu.SemaphoreType.DMA((peers,)),
-            pltpu.SemaphoreType.DMA((peers,)),
-            pltpu.SemaphoreType.DMA((peers,)),
-            pltpu.SemaphoreType.DMA((peers,)),
+            pltpu.VMEM((rows, columns), bf16),
+            pltpu.VMEM((peers, depth, width), bf16),
+            pltpu.VMEM((half, rows, width), jnp.float32),
+            pltpu.VMEM((half, rows, width), bf16),
+            pltpu.VMEM((half, rows, width), bf16),
+            dma((8,)),
+            dma((peers,)),
+            dma((peers,)),
+            dma((peers,)),
+            dma((peers,)),
+            dma((peers, 4)),
+            dma((peers,)),
+            dma((half,)),
+            dma((half,)),
         ],
         compiler_params=pltpu.CompilerParams(
-            collective_id=0, has_side_effects=True, vmem_limit_bytes=48 * 1024 * 1024
+            collective_id=0, has_side_effects=True, vmem_limit_bytes=58 * 1024 * 1024
         ),
         cost_estimate=pl.CostEstimate(
-            flops=40 * 1024 * 1024 * slots * chans // 8,
+            flops=2 * rows * depth * width * peers,
             bytes_accessed=16 * 1024 * 1024,
             transcendentals=0,
         ),
-    )(k_feat, v_feat, q_feat, filters, *[jnp.asarray(t) for t in tables])
+    )(k_feat, v_feat, q_feat, stream, filters, w_out, *[jnp.asarray(t) for t in tables])
 
 
 def gated_features(q_feat, k_feat, v_feat, filters):
-    peers = lax.axis_size("seq")
-    if filters.shape[0] == LANES and q_feat.shape[0] % LANES == 0:
-        return gated_mixer(q_feat, k_feat, v_feat, filters, peers)
     mixed = (k_feat.astype(jnp.float32) * v_feat.astype(jnp.float32)).astype(jnp.bfloat16)
     sent_mixed = lax.all_to_all(mixed.T, "seq", split_axis=0, concat_axis=1, tiled=True)
     conv_out = long_conv(sent_mixed, filters).astype(jnp.bfloat16)
@@ -357,6 +575,15 @@
 
 
 def local(q_feat, k_feat, v_feat, stream, filters, w_out):
+    peers = lax.axis_size("seq")
+    if (
+        filters.shape[0] == LANES
+        and q_feat.shape[0] % LANES == 0
+        and peers % 4 == 0
+        and lax.axis_size("tp") == 2
+        and w_out.shape[1] % LANES == 0
+    ):
+        return fused_mixer(q_feat, k_feat, v_feat, stream, filters, w_out, peers)
     gated = gated_features(q_feat, k_feat, v_feat, filters)
     terms = jnp.dot(
         gated, lax.all_gather(w_out, "seq", axis=1, tiled=True), preferred_element_type=jnp.float32

time: 231 us -> 160 us (0.69)
  waiting for transfers between devices: 111 us -> 0 us
  Pallas kernels: 85.8 us -> 158 us
  between operations: 13.4 us -> 0.01 us
  matrix products: 11.5 us -> 0 us
  local copies, waits for them, and re-layouts: 4.9 us -> 2.3 us
  other arithmetic: 2.58 us -> 0 us
    all_gather x1 -> x0, waiting for transfers between devices: 78.5 us -> none  [local(): lax.all_gather(w_out, 'seq', axis=1, tiled=True)]
    pallas_call x1, Pallas kernels: 85.8 us -> 158 us  [fused_mixer(): pl.pallas_call(functools.partial(mixer_kernel, peers), out_shape=jax.Shap...]
    reduce_scatter x1 -> x0, waiting for transfers between devices: 32 us -> none  [local(): lax.psum_scatter(terms.astype(jnp.bfloat16), 'tp', scatter_dimension=1, t...]
    dot_general x1 -> x0, matrix products: 11.5 us -> none  [local(): jnp.dot(gated, lax.all_gather(w_out, 'seq', axis=1, tiled=True), preferre...]
    unnamed x10 -> x1, local copies, waits for them, and re-layouts: 4.9 us -> 2.3 us
    convert_element_type x1 -> x0, other arithmetic: 2.58 us -> none  [local(): return (stream.astype(jnp.float32) + accumulated_total).astype(jnp.bfloat16)]
  transfers between devices with their start and end apart: 2 -> 0, of which waited for: 2 -> 0; matrix products, arithmetic and copies ran while one was open for 0% -> 0% of each run, Pallas kernels for 37% -> 0%
where the time goes in v1:
time: 160 us
  Pallas kernels  158 us (99%)
  local copies, waits for them, and re-layouts  2.3 us (1%)
    pallas_call x1, Pallas kernels, fused_mixer(): pl.pallas_call(functools.partial(mixer_kernel, peers), out_shape=jax.Shap...  158 us

profile of v1, /device:TPU:18, one launch (start us, length us, event | category | flops | bytes accessed | tf_op | source)
XLA Modules:
  0.0 160.3 jit_solution(3948593088314227623)
XLA Ops:
  0.0 157.9 %shard_map.100 = bf16[256,2048]{1,0:T(8,128)(2,1)} custom-call(bf16[256,2048]{1,0:T(8,128)(2,1)} %k_ref.1, bf16[256,2048]{1,0:T(8,128)(2,1)} %v_ref.1, bf16[256,2048]{1,0:T(8,128)(2,1)} %q_hbm.1, bf16[256,2048]{1,0:T(8,128)(2,1)} %stream_hbm.1, f32[128,4096]{1,0:T(8,128)} %taps_hbm.1, bf16[2048,256]{1,0:T(8,128)(2,1)} %weights_hbm.1, ...), custom_call_target="tpu_custom_call" | custom-call | flops 4294967296 | bytes 16777216 | tf_op jit(solution)/shard_map/pallas_call | solution.py:522
  158.0 2.3 %copy.12 = bf16[256,2048]{1,0:T(8,128)(2,1)} copy(bf16[256,2048]{1,0:T(8,128)(2,1)} %shard_map.100) | data formatting | bytes 2097152

commit v2 on v1

--- a/solution.py
+++ b/solution.py
@@ -11,6 +11,7 @@
 
 LANES = 128
 GROUP = 16
+PIECES = 4
 
 def window_extent(total):
     chosen = 2
@@ -215,12 +216,15 @@
     def block_at(zz, xx, cc):
         return (zz * 2 + xx) * 2 + cc
 
-    def weight_copy(block, target, way):
+    piece = weights.shape[1] // PIECES
+
+    def weight_copy(block, part, target, way):
+        held = weights.at[block, pl.ds(part * piece, piece)]
         return pltpu.make_async_remote_copy(
-            src_ref=weights.at[block],
-            dst_ref=weights.at[block],
-            send_sem=send_weight.at[block, way],
-            recv_sem=recv_weight.at[block],
+            src_ref=held,
+            dst_ref=held,
+            send_sem=send_weight.at[block * PIECES + part, way],
+            recv_sem=recv_weight.at[block * PIECES + part],
             device_id={"seq": target},
             device_id_type=mesh_ids,
         )
@@ -234,24 +238,24 @@
         else:
             copy.wait_send()
 
-    def spread(block, sending, up, down):
+    def spread(block, part, sending, up, down):
         if up:
 
             @pl.when(layer + 1 < depth)
             def _():
-                act(weight_copy(block, me + 4, 2), sending)
+                act(weight_copy(block, part, me + 4, 2), sending)
 
         if down:
 
             @pl.when(layer > 0)
             def _():
-                act(weight_copy(block, me - 4, 3), sending)
-
-        act(weight_copy(block, to_side, 1), sending)
-        act(weight_copy(block, to_core, 0), sending)
-
-    def arrive(block):
-        weight_copy(block, to_core, 0).wait_recv()
+                act(weight_copy(block, part, me - 4, 3), sending)
+
+        act(weight_copy(block, part, to_side, 1), sending)
+        act(weight_copy(block, part, to_core, 0), sending)
+
+    def arrive(block, part):
+        weight_copy(block, part, to_core, 0).wait_recv()
 
     def at_distance(d, body):
         for sign in (-1, 1) if d else (1,):
@@ -261,27 +265,29 @@
             def _():
                 body(zz, sign)
 
-    def from_layer(d):
+    def from_layer(d, *parts):
         if d >= depth:
             return
 
-        def body(zz, sign):
+        def body(zz, sign, part):
             block = block_at(zz, side, core)
-            arrive(block)
-            spread(block, True, sign < 0, sign > 0)
-
-        at_distance(d, body)
-
-    def from_side(d):
+            arrive(block, part)
+            spread(block, part, True, sign < 0, sign > 0)
+
+        for part in parts or range(PIECES):
+            at_distance(d, functools.partial(body, part=part))
+
+    def from_side(d, *parts):
         if d >= depth:
             return
 
-        def body(zz, sign):
+        def body(zz, sign, part):
             block = block_at(zz, 1 - side, core)
-            arrive(block)
-            weight_copy(block, to_core, 0).start()
-
-        at_distance(d, body)
+            arrive(block, part)
+            weight_copy(block, part, to_core, 0).start()
+
+        for part in parts or range(PIECES):
+            at_distance(d, functools.partial(body, part=part))
 
     def share_copy(b):
         return pltpu.make_async_remote_copy(
@@ -296,7 +302,8 @@
     def project(d):
         def body(zz, sign):
             for xx in (0, 1):
-                arrive(block_at(zz, xx, 1 - core))
+                for part in range(PIECES):
+                    arrive(block_at(zz, xx, 1 - core), part)
 
             def step(i, carry):
                 block = zz * 4 + i
@@ -353,7 +360,8 @@
         first_copies.append(copy)
     signal[pl.ds(me * per, per)] = sent[me]
     loads[0].wait()
-    spread(me, True, True, True)
+    for part in range(PIECES):
+        spread(me, part, True, True, True)
 
     def outer_stage(source):
         def step(g, carry):
@@ -391,17 +399,19 @@
     loads[2].wait()
     outer_stage(turned)
     loads[3].wait()
+    from_layer(1, 0)
 
     def tap_step(s, carry):
         spectrum[s] = inner_forward(s)
         return carry
 
     lax.fori_loop(0, slots, tap_step, 0, unroll=2)
+    from_layer(1, 1)
 
     for copy in first_copies:
         copy.wait_recv()
     outer_stage(signal)
-    from_layer(1)
+    from_layer(1, 2, 3)
     loads[4].wait()
 
     def middle(s, slot_zero):
@@ -415,7 +425,10 @@
         middle(s, False)
         return carry
 
-    lax.fori_loop(1, slots, middle_step, 0, unroll=2)
+    lax.fori_loop(1, slots // 2, middle_step, 0, unroll=2)
+    from_layer(2, 0)
+    lax.fori_loop(slots // 2, slots, middle_step, 0, unroll=2)
+    from_layer(2, 1)
 
     loads[5].wait()
 
@@ -451,8 +464,9 @@
         copy.start()
         second_copies.append(copy)
     from_side(0)
-    from_layer(2)
+    from_layer(2, 2, 3)
     from_side(1)
+    from_layer(3, 0, 1)
     loads[6].wait()
 
     def gate(p, block):
@@ -465,8 +479,8 @@
         copy.wait_recv()
         source = lax.rem(me + peers - i, peers)
         gate(source, returned[source])
+    from_layer(3, 2, 3)
     project(0)
-    from_layer(3)
     from_side(2)
     project(1)
     project(2)
@@ -490,13 +504,15 @@
 
     for copy in first_copies + second_copies:
         copy.wait_send()
-    spread(me, False, True, True)
+    for part in range(PIECES):
+        spread(me, part, False, True, True)
     for d in range(depth):
 
         def settle(zz, sign):
-            if d:
-                spread(block_at(zz, side, core), False, sign < 0, sign > 0)
-            weight_copy(block_at(zz, 1 - side, core), to_core, 0).wait_send()
+            for part in range(PIECES):
+                if d:
+                    spread(block_at(zz, side, core), part, False, sign < 0, sign > 0)
+                weight_copy(block_at(zz, 1 - side, core), part, to_core, 0).wait_send()
 
         at_distance(d, settle)
 
@@ -548,8 +564,8 @@
             dma((peers,)),
             dma((peers,)),
             dma((peers,)),
-            dma((peers, 4)),
-            dma((peers,)),
+            dma((peers * PIECES, 4)),
+            dma((peers * PIECES,)),
             dma((half,)),
             dma((half,)),
         ],

time: 160 us -> 152 us (0.950); the launches traced: 160 us -> 150 us
  Pallas kernels: 158 us -> 148 us
    pallas_call x1, Pallas kernels: 158 us -> 148 us  [fused_mixer(): pl.pallas_call(functools.partial(mixer_kernel, peers), out_shape=jax.Shap...]
where the time goes in v2:
time: 152 us; the launch traced here: 150 us
  Pallas kernels  148 us (97%)
  local copies, waits for them, and re-layouts  2.3 us (2%)
    pallas_call x1, Pallas kernels, fused_mixer(): pl.pallas_call(functools.partial(mixer_kernel, peers), out_shape=jax.Shap...  148 us

profile of v2, /device:TPU:18, one launch (start us, length us, event | category | flops | bytes accessed | tf_op | source)
XLA Modules:
  0.0 150.3 jit_solution(8231497513743375939)
XLA Ops:
  0.0 148.0 %shard_map.100 = bf16[256,2048]{1,0:T(8,128)(2,1)} custom-call(bf16[256,2048]{1,0:T(8,128)(2,1)} %k_ref.1, bf16[256,2048]{1,0:T(8,128)(2,1)} %v_ref.1, bf16[256,2048]{1,0:T(8,128)(2,1)} %q_hbm.1, bf16[256,2048]{1,0:T(8,128)(2,1)} %stream_hbm.1, f32[128,4096]{1,0:T(8,128)} %taps_hbm.1, bf16[2048,256]{1,0:T(8,128)(2,1)} %weights_hbm.1, ...), custom_call_target="tpu_custom_call" | custom-call | flops 4294967296 | bytes 16777216 | tf_op jit(solution)/shard_map/pallas_call | solution.py:538
  148.0 2.3 %copy.12 = bf16[256,2048]{1,0:T(8,128)(2,1)} copy(bf16[256,2048]{1,0:T(8,128)(2,1)} %shard_map.100) | data formatting | bytes 2097152

commit v3 on v2

--- a/solution.py
+++ b/solution.py
@@ -174,6 +174,8 @@
     kept,
     shares,
     arrived,
+    passed,
+    handed,
     load_sem,
     send_one,
     recv_one,
@@ -183,6 +185,10 @@
     recv_weight,
     send_share,
     recv_share,
+    send_gated,
+    recv_gated,
+    send_passed,
+    recv_passed,
 ):
     me = lax.axis_index("seq")
     tp = lax.axis_index("tp")
@@ -192,14 +198,14 @@
     total = 2 * slots * LANES
     mesh_ids = pl.DeviceIdType.MESH
     depth = peers // 4
-    half = peers // 2
+    width = weights.shape[2]
     layer, side, core = me // 4, (me // 2) % 2, me % 2
 
     loads = [
         pltpu.make_async_copy(source, target, load_sem.at[i])
         for i, (source, target) in enumerate(
             [
-                (weights_hbm, weights.at[me]),
+                (weights_hbm, weights.at[layer * 2 + core]),
                 (taps_hbm, taps_ref),
                 (outer_hbm, outer_ref),
                 (inner_hbm, inner_ref),
@@ -212,9 +218,6 @@
     ]
     for load in loads:
         load.start()
-
-    def block_at(zz, xx, cc):
-        return (zz * 2 + xx) * 2 + cc
 
     piece = weights.shape[1] // PIECES
 
@@ -229,8 +232,9 @@
             device_id_type=mesh_ids,
         )
 
-    to_core = block_at(layer, side, 1 - core)
-    to_side = block_at(layer, 1 - side, core)
+    to_core = (layer * 2 + side) * 2 + 1 - core
+    to_side = (layer * 2 + 1 - side) * 2 + core
+    mine = layer * 2 + core
 
     def act(copy, sending):
         if sending:
@@ -243,15 +247,14 @@
 
             @pl.when(layer + 1 < depth)
             def _():
-                act(weight_copy(block, part, me + 4, 2), sending)
+                act(weight_copy(block, part, me + 4, 1), sending)
 
         if down:
 
             @pl.when(layer > 0)
             def _():
-                act(weight_copy(block, part, me - 4, 3), sending)
-
-        act(weight_copy(block, part, to_side, 1), sending)
+                act(weight_copy(block, part, me - 4, 2), sending)
+
         act(weight_copy(block, part, to_core, 0), sending)
 
     def arrive(block, part):
@@ -270,21 +273,9 @@
             return
 
         def body(zz, sign, part):
-            block = block_at(zz, side, core)
+            block = zz * 2 + core
             arrive(block, part)
             spread(block, part, True, sign < 0, sign > 0)
-
-        for part in parts or range(PIECES):
-            at_distance(d, functools.partial(body, part=part))
-
-    def from_side(d, *parts):
-        if d >= depth:
-            return
-
-        def body(zz, sign, part):
-            block = block_at(zz, 1 - side, core)
-            arrive(block, part)
-            weight_copy(block, part, to_core, 0).start()
 
         for part in parts or range(PIECES):
             at_distance(d, functools.partial(body, part=part))
@@ -299,29 +290,74 @@
             device_id_type=mesh_ids,
         )
 
+    def gated_copy(p):
+        cols = pl.ds(pl.multiple_of(p * LANES, LANES), LANES)
+        return pltpu.make_async_remote_copy(
+            src_ref=gated.at[0, :, cols],
+            dst_ref=gated.at[1, :, cols],
+            send_sem=send_gated.at[p],
+            recv_sem=recv_gated.at[p],
+            device_id={"seq": to_side},
+            device_id_type=mesh_ids,
+        )
+
+    def passed_copy(b):
+        return pltpu.make_async_remote_copy(
+            src_ref=passed.at[b],
+            dst_ref=handed.at[b],
+            send_sem=send_passed.at[b],
+            recv_sem=recv_passed.at[b],
+            device_id={"seq": to_side},
+            device_id_type=mesh_ids,
+        )
+
     def project(d):
         def body(zz, sign):
-            for xx in (0, 1):
-                for part in range(PIECES):
-                    arrive(block_at(zz, xx, 1 - core), part)
+            for part in range(PIECES):
+                arrive(zz * 2 + 1 - core, part)
 
             def step(i, carry):
-                block = zz * 4 + i
-                terms = jnp.dot(gated[...], weights[block], preferred_element_type=jnp.float32)
-                b = block % half
-
-                @pl.when(block // half == tp)
+                block = zz * 2 + i
+                terms = jnp.dot(
+                    gated[...].reshape(2 * rows, gated.shape[2]),
+                    weights[block],
+                    preferred_element_type=jnp.float32,
+                )
+                b = block % depth
+
+                @pl.when(block // depth == tp)
                 def _():
                     kept[b] = terms
 
-                @pl.when(block // half != tp)
+                @pl.when(block // depth != tp)
                 def _():
                     shares[b] = terms.astype(jnp.bfloat16)
                     share_copy(b).start()
 
                 return carry
 
-            lax.fori_loop(0, 4, step, 0)
+            lax.fori_loop(0, 2, step, 0)
+
+        if d < depth:
+            at_distance(d, body)
+
+    def place(b, xx, values):
+        spot = (b // 2) * 4 + xx * 2 + b % 2
+        cols = pl.ds(pl.multiple_of(spot * width, width), width)
+        out_ref[:, cols] = (stream_ref[:, cols].astype(jnp.float32) + values).astype(jnp.bfloat16)
+
+    def finish(d):
+        def body(zz, sign):
+            @pl.when(zz * 2 // depth == tp)
+            def _():
+                for i in (0, 1):
+                    b = zz * 2 + i - tp * depth
+                    share_copy(b).wait_recv()
+                    passed[b] = (
+                        kept[b, rows:, :] + arrived[b, rows:, :].astype(jnp.float32)
+                    ).astype(jnp.bfloat16)
+                    passed_copy(b).start()
+                    place(b, side, kept[b, :rows, :] + arrived[b, :rows, :].astype(jnp.float32))
 
         if d < depth:
             at_distance(d, body)
@@ -361,7 +397,7 @@
     signal[pl.ds(me * per, per)] = sent[me]
     loads[0].wait()
     for part in range(PIECES):
-        spread(me, part, True, True, True)
+        spread(mine, part, True, True, True)
 
     def outer_stage(source):
         def step(g, carry):
@@ -463,64 +499,74 @@
         )
         copy.start()
         second_copies.append(copy)
-    from_side(0)
     from_layer(2, 2, 3)
-    from_side(1)
-    from_layer(3, 0, 1)
     loads[6].wait()
 
     def gate(p, block):
         cols = pl.ds(pl.multiple_of(p * LANES, LANES), LANES)
         conv = block.reshape(rows, LANES).astype(jnp.float32)
-        gated[:, cols] = (q_ref[:, cols].astype(jnp.float32) * conv).astype(jnp.bfloat16)
+        gated[0, :, cols] = (q_ref[:, cols].astype(jnp.float32) * conv).astype(jnp.bfloat16)
+        gated_copy(p).start()
 
     gate(me, result[pl.ds(me * per, per)])
     for i, copy in enumerate(second_copies, 1):
         copy.wait_recv()
         source = lax.rem(me + peers - i, peers)
         gate(source, returned[source])
+    loads[7].wait()
+    from_layer(3, 0, 1)
+
+    def gated_in(p, carry):
+        gated_copy(p).wait_recv()
+        return carry
+
+    lax.fori_loop(0, peers, gated_in, 0)
+    project(0)
+    project(1)
+    finish(0)
+    project(2)
+    finish(1)
     from_layer(3, 2, 3)
-    project(0)
-    from_side(2)
-    project(1)
-    project(2)
-    for d in range(3, depth):
-        if d > 3:
-            from_layer(d)
-        from_side(d)
+    project(3)
+    finish(2)
+    for d in range(4, depth):
+        from_layer(d)
         project(d)
-
-    loads[7].wait()
-    width = kept.shape[2]
-
-    def finish(b, carry):
-        share_copy(b).wait_recv()
-        cols = pl.ds(pl.multiple_of(b * width, width), width)
-        added = kept[b] + arrived[b].astype(jnp.float32)
-        out_ref[:, cols] = (stream_ref[:, cols].astype(jnp.float32) + added).astype(jnp.bfloat16)
-        return carry
-
-    lax.fori_loop(0, half, finish, 0)
+        finish(d - 1)
+    if depth > 3:
+        finish(depth - 1)
+
+    def place_handed(b, carry):
+        passed_copy(b).wait_recv()
+        place(b, 1 - side, handed[b].astype(jnp.float32))
+        return carry
+
+    lax.fori_loop(0, depth, place_handed, 0)
 
     for copy in first_copies + second_copies:
         copy.wait_send()
     for part in range(PIECES):
-        spread(me, part, False, True, True)
-    for d in range(depth):
+        spread(mine, part, False, True, True)
+    for d in range(1, depth):
 
         def settle(zz, sign):
             for part in range(PIECES):
-                if d:
-                    spread(block_at(zz, side, core), part, False, sign < 0, sign > 0)
-                weight_copy(block_at(zz, 1 - side, core), part, to_core, 0).wait_send()
+                spread(zz * 2 + core, part, False, sign < 0, sign > 0)
 
         at_distance(d, settle)
+
+    def sent_gated(p, carry):
+        gated_copy(p).wait_send()
+        return carry
+
+    lax.fori_loop(0, peers, sent_gated, 0)
 
     def sent_share(b, carry):
         share_copy(b).wait_send()
-        return carry
-
-    lax.fori_loop(0, half, sent_share, 0)
+        passed_copy(b).wait_send()
+        return carry
+
+    lax.fori_loop(0, depth, sent_share, 0)
 
 
 def fused_mixer(q_feat, k_feat, v_feat, stream, filters, w_out, peers):
@@ -532,8 +578,8 @@
     vmem = pl.BlockSpec(memory_space=pltpu.VMEM)
     anywhere = pl.BlockSpec(memory_space=pl.ANY)
     bf16 = jnp.bfloat16
-    depth, width = w_out.shape
-    half = peers // 2
+    inner, width = w_out.shape
+    depth = peers // 4
     dma = pltpu.SemaphoreType.DMA
     return pl.pallas_call(
         functools.partial(mixer_kernel, peers),
@@ -554,26 +600,32 @@
             pltpu.VMEM((slots, LANES, LANES), bf16),
             pltpu.VMEM((slots, 2 * LANES, LANES), jnp.float32),
             pltpu.VMEM((slots, 2, LANES, LANES), bf16),
-            pltpu.VMEM((rows, columns), bf16),
-            pltpu.VMEM((peers, depth, width), bf16),
-            pltpu.VMEM((half, rows, width), jnp.float32),
-            pltpu.VMEM((half, rows, width), bf16),
-            pltpu.VMEM((half, rows, width), bf16),
+            pltpu.VMEM((2, rows, columns), bf16),
+            pltpu.VMEM((2 * depth, inner, width), bf16),
+            pltpu.VMEM((depth, 2 * rows, width), jnp.float32),
+            pltpu.VMEM((depth, 2 * rows, width), bf16),
+            pltpu.VMEM((depth, 2 * rows, width), bf16),
+            pltpu.VMEM((depth, rows, width), bf16),
+            pltpu.VMEM((depth, rows, width), bf16),
             dma((8,)),
             dma((peers,)),
             dma((peers,)),
             dma((peers,)),
             dma((peers,)),
-            dma((peers * PIECES, 4)),
-            dma((peers * PIECES,)),
-            dma((half,)),
-            dma((half,)),
+            dma((2 * depth * PIECES, 3)),
+            dma((2 * depth * PIECES,)),
+            dma((depth,)),
+            dma((depth,)),
+            dma((peers,)),
+            dma((peers,)),
+            dma((depth,)),
+            dma((depth,)),
         ],
         compiler_params=pltpu.CompilerParams(
             collective_id=0, has_side_effects=True, vmem_limit_bytes=58 * 1024 * 1024
         ),
         cost_estimate=pl.CostEstimate(
-            flops=2 * rows * depth * width * peers,
+            flops=2 * rows * inner * width * peers,
             bytes_accessed=16 * 1024 * 1024,
             transcendentals=0,
         ),
@@ -595,7 +647,7 @@
     if (
         filters.shape[0] == LANES
         and q_feat.shape[0] % LANES == 0
-        and peers % 4 == 0
+        and peers % 8 == 0
         and lax.axis_size("tp") == 2
         and w_out.shape[1] % LANES == 0
     ):

time: 152 us -> 164 us (1.079)
  the two profiles are of different devices: /device:TPU:18 before, /device:TPU:25 now
where the time goes in v3:
time: 164 us
  Pallas kernels  161 us (98%)
  local copies, waits for them, and re-layouts  2.3 us (1%)
    pallas_call x1, Pallas kernels, fused_mixer(): pl.pallas_call(functools.partial(mixer_kernel, peers), out_shape=jax.Shap...  161 us

profile of v3, /device:TPU:25, one launch (start us, length us, event | category | flops | bytes accessed | tf_op | source)
XLA Modules:
  0.0 163.6 jit_solution(3029499824466944968)
XLA Ops:
  0.0 161.3 %shard_map.100 = bf16[256,2048]{1,0:T(8,128)(2,1)} custom-call(bf16[256,2048]{1,0:T(8,128)(2,1)} %k_ref.1, bf16[256,2048]{1,0:T(8,128)(2,1)} %v_ref.1, bf16[256,2048]{1,0:T(8,128)(2,1)} %q_hbm.1, bf16[256,2048]{1,0:T(8,128)(2,1)} %stream_hbm.1, f32[128,4096]{1,0:T(8,128)} %taps_hbm.1, bf16[2048,256]{1,0:T(8,128)(2,1)} %weights_hbm.1, ...), custom_call_target="tpu_custom_call" | custom-call | flops 4294967296 | bytes 16777216 | tf_op jit(solution)/shard_map/pallas_call | solution.py:584
  161.3 2.3 %copy.12 = bf16[256,2048]{1,0:T(8,128)(2,1)} copy(bf16[256,2048]{1,0:T(8,128)(2,1)} %shard_map.100) | data formatting | bytes 2097152

commit v4 on v2

--- a/solution.py
+++ b/solution.py
@@ -193,6 +193,7 @@
     mesh_ids = pl.DeviceIdType.MESH
     depth = peers // 4
     half = peers // 2
+    width = weights.shape[2]
     layer, side, core = me // 4, (me // 2) % 2, me % 2
 
     loads = [
@@ -299,14 +300,14 @@
             device_id_type=mesh_ids,
         )
 
-    def project(d):
-        def body(zz, sign):
-            for xx in (0, 1):
-                for part in range(PIECES):
-                    arrive(block_at(zz, xx, 1 - core), part)
+    def project(d, turns=(0, 1)):
+        def body(zz, sign, turn):
+            xx = side if turn == 0 else 1 - side
+            for part in range(PIECES):
+                arrive(block_at(zz, xx, 1 - core), part)
 
             def step(i, carry):
-                block = zz * 4 + i
+                block = block_at(zz, xx, i)
                 terms = jnp.dot(gated[...], weights[block], preferred_element_type=jnp.float32)
                 b = block % half
 
@@ -321,7 +322,26 @@
 
                 return carry
 
-            lax.fori_loop(0, 4, step, 0)
+            lax.fori_loop(0, 2, step, 0)
+
+        if d < depth:
+            for turn in turns:
+                at_distance(d, functools.partial(body, turn=turn))
+
+    def finish(d):
+        def body(zz, sign):
+            @pl.when(zz * 4 // half == tp)
+            def _():
+                def step(i, carry):
+                    b = (zz * 4 + i) % half
+                    share_copy(b).wait_recv()
+                    cols = pl.ds(pl.multiple_of(b * width, width), width)
+                    added = kept[b] + arrived[b].astype(jnp.float32)
+                    total = stream_ref[:, cols].astype(jnp.float32) + added
+                    out_ref[:, cols] = total.astype(jnp.bfloat16)
+                    return carry
+
+                lax.fori_loop(0, 4, step, 0)
 
         if d < depth:
             at_distance(d, body)
@@ -360,7 +380,7 @@
         first_copies.append(copy)
     signal[pl.ds(me * per, per)] = sent[me]
     loads[0].wait()
-    for part in range(PIECES):
+    for part in range(PIECES // 2):
         spread(me, part, True, True, True)
 
     def outer_stage(source):
@@ -399,14 +419,15 @@
     loads[2].wait()
     outer_stage(turned)
     loads[3].wait()
-    from_layer(1, 0)
+    for part in range(PIECES // 2, PIECES):
+        spread(me, part, True, True, True)
 
     def tap_step(s, carry):
         spectrum[s] = inner_forward(s)
         return carry
 
-    lax.fori_loop(0, slots, tap_step, 0, unroll=2)
-    from_layer(1, 1)
+    lax.fori_loop(0, slots, tap_step, 0, unroll=4)
+    from_layer(1, 0, 1)
 
     for copy in first_copies:
         copy.wait_recv()
@@ -425,9 +446,9 @@
         middle(s, False)
         return carry
 
-    lax.fori_loop(1, slots // 2, middle_step, 0, unroll=2)
+    lax.fori_loop(1, slots // 2, middle_step, 0, unroll=4)
     from_layer(2, 0)
-    lax.fori_loop(slots // 2, slots, middle_step, 0, unroll=2)
+    lax.fori_loop(slots // 2, slots, middle_step, 0, unroll=4)
     from_layer(2, 1)
 
     loads[5].wait()
@@ -466,8 +487,10 @@
     from_side(0)
     from_layer(2, 2, 3)
     from_side(1)
-    from_layer(3, 0, 1)
+    from_layer(3)
+    from_side(2)
     loads[6].wait()
+    loads[7].wait()
 
     def gate(p, block):
         cols = pl.ds(pl.multiple_of(p * LANES, LANES), LANES)
@@ -479,28 +502,22 @@
         copy.wait_recv()
         source = lax.rem(me + peers - i, peers)
         gate(source, returned[source])
-    from_layer(3, 2, 3)
     project(0)
-    from_side(2)
     project(1)
+    finish(0)
     project(2)
-    for d in range(3, depth):
-        if d > 3:
-            from_layer(d)
+    finish(1)
+    project(3, (0,))
+    from_side(3)
+    project(3, (1,))
+    finish(2)
+    for d in range(4, depth):
+        from_layer(d)
         from_side(d)
         project(d)
-
-    loads[7].wait()
-    width = kept.shape[2]
-
-    def finish(b, carry):
-        share_copy(b).wait_recv()
-        cols = pl.ds(pl.multiple_of(b * width, width), width)
-        added = kept[b] + arrived[b].astype(jnp.float32)
-        out_ref[:, cols] = (stream_ref[:, cols].astype(jnp.float32) + added).astype(jnp.bfloat16)
-        return carry
-
-    lax.fori_loop(0, half, finish, 0)
+        finish(d - 1)
+    if depth > 3:
+        finish(depth - 1)
 
     for copy in first_copies + second_copies:
         copy.wait_send()
@@ -595,7 +612,7 @@
     if (
         filters.shape[0] == LANES
         and q_feat.shape[0] % LANES == 0
-        and peers % 4 == 0
+        and peers % 8 == 0
         and lax.axis_size("tp") == 2
         and w_out.shape[1] % LANES == 0
     ):

time: 152 us -> 155 us (1.020)
  Pallas kernels: 148 us -> 150 us
    pallas_call x1, Pallas kernels: 148 us -> 150 us  [fused_mixer(): pl.pallas_call(functools.partial(mixer_kernel, peers), out_shape=jax.Shap...]
where the time goes in v4:
time: 155 us; the launch traced here: 153 us
  Pallas kernels  150 us (97%)
  local copies, waits for them, and re-layouts  2.3 us (1%)
    pallas_call x1, Pallas kernels, fused_mixer(): pl.pallas_call(functools.partial(mixer_kernel, peers), out_shape=jax.Shap...  150 us

profile of v4, /device:TPU:18, one launch (start us, length us, event | category | flops | bytes accessed | tf_op | source)
XLA Modules:
  0.0 152.6 jit_solution(11321370702573716421)
XLA Ops:
  0.0 150.3 %shard_map.100 = bf16[256,2048]{1,0:T(8,128)(2,1)} custom-call(bf16[256,2048]{1,0:T(8,128)(2,1)} %k_ref.1, bf16[256,2048]{1,0:T(8,128)(2,1)} %v_ref.1, bf16[256,2048]{1,0:T(8,128)(2,1)} %q_hbm.1, bf16[256,2048]{1,0:T(8,128)(2,1)} %stream_hbm.1, f32[128,4096]{1,0:T(8,128)} %taps_hbm.1, bf16[2048,256]{1,0:T(8,128)(2,1)} %weights_hbm.1, ...), custom_call_target="tpu_custom_call" | custom-call | flops 4294967296 | bytes 16777216 | tf_op jit(solution)/shard_map/pallas_call | solution.py:555
  150.3 2.3 %copy.12 = bf16[256,2048]{1,0:T(8,128)(2,1)} copy(bf16[256,2048]{1,0:T(8,128)(2,1)} %shard_map.100) | data formatting | bytes 2097152

commit v5 on v4

--- a/solution.py
+++ b/solution.py
@@ -362,8 +362,11 @@
         sent[p] = product.astype(jnp.bfloat16).reshape(per, LANES, LANES)
         return carry
 
+    loads[0].wait()
+    pl.semaphore_wait(barrier, peers)
+    for part in range(PIECES):
+        spread(me, part, True, True, True)
     lax.fori_loop(0, peers, mix, 0)
-    pl.semaphore_wait(barrier, peers)
 
     first_copies = []
     for i in range(1, peers):
@@ -379,9 +382,6 @@
         copy.start()
         first_copies.append(copy)
     signal[pl.ds(me * per, per)] = sent[me]
-    loads[0].wait()
-    for part in range(PIECES // 2):
-        spread(me, part, True, True, True)
 
     def outer_stage(source):
         def step(g, carry):
@@ -419,15 +419,14 @@
     loads[2].wait()
     outer_stage(turned)
     loads[3].wait()
-    for part in range(PIECES // 2, PIECES):
-        spread(me, part, True, True, True)
+    from_layer(1, 0)
 
     def tap_step(s, carry):
         spectrum[s] = inner_forward(s)
         return carry
 
     lax.fori_loop(0, slots, tap_step, 0, unroll=4)
-    from_layer(1, 0, 1)
+    from_layer(1, 1)
 
     for copy in first_copies:
         copy.wait_recv()

time: 155 us -> 154 us (level)
  no operation moved by 1% of the time
where the time goes in v5:
time: 154 us; the launch traced here: 153 us
  Pallas kernels  150 us (97%)
  local copies, waits for them, and re-layouts  2.3 us (1%)
    pallas_call x1, Pallas kernels, fused_mixer(): pl.pallas_call(functools.partial(mixer_kernel, peers), out_shape=jax.Shap...  150 us

profile of v5, /device:TPU:18, one launch (start us, length us, event | category | flops | bytes accessed | tf_op | source)
XLA Modules:
  0.0 152.6 jit_solution(15342235227430467113)
XLA Ops:
  0.0 150.3 %shard_map.100 = bf16[256,2048]{1,0:T(8,128)(2,1)} custom-call(bf16[256,2048]{1,0:T(8,128)(2,1)} %k_ref.1, bf16[256,2048]{1,0:T(8,128)(2,1)} %v_ref.1, bf16[256,2048]{1,0:T(8,128)(2,1)} %q_hbm.1, bf16[256,2048]{1,0:T(8,128)(2,1)} %stream_hbm.1, f32[128,4096]{1,0:T(8,128)} %taps_hbm.1, bf16[2048,256]{1,0:T(8,128)(2,1)} %weights_hbm.1, ...), custom_call_target="tpu_custom_call" | custom-call | flops 4294967296 | bytes 16777216 | tf_op jit(solution)/shard_map/pallas_call | solution.py:554
  150.3 2.3 %copy.12 = bf16[256,2048]{1,0:T(8,128)(2,1)} copy(bf16[256,2048]{1,0:T(8,128)(2,1)} %shard_map.100) | data formatting | bytes 2097152
